TPU v7x, 32 devices: a whole 2x2x4 slice. The times are simulated.
32 devices in a mesh: dp: 4 (over y, x), expert: 8 (over z, core).
Axes of the slice: x: 2, y: 2, z: 4, core: 2. Of those that a mesh axis runs over, the one named last changes fastest.
Arguments:
- tokens: bfloat16 [4096, 1024], P(('dp', 'expert')), may hold values from -6 to 6
- upstream: bfloat16 [4096, 1024], P(('dp', 'expert')), may hold values from -6 to 6
- task_ids: int32 [4096, 1], P(('dp', 'expert')), may hold values from 0 to 7; in each aligned block of 128 rows (0 to 127, 128 to 255, ...) at most 18 rows name the same one
- task_expert: int32 [8], replicated, may hold values from 0 to 7, each once
- w_in: bfloat16 [8, 1024, 4096], P('expert', None, 'dp'), may hold values from -0.1875 to 0.1875
- w_out: bfloat16 [8, 4096, 1024], P('expert', 'dp'), may hold values from -0.09375 to 0.09375
Outputs:
- token_grad: bfloat16 [4096, 1024], P(('dp', 'expert'))
- grad_in: float32 [8, 1024, 4096], P('expert', None, 'dp')
- grad_out: float32 [8, 4096, 1024], P('expert', 'dp')
Inputs may be any that keep to these rules, and one draw needn't show every extreme that they name: `task_ids`: among the 128 rows of one device no task appears more than 18 times, and some task appears exactly 18 times in the rows of some device. `task_expert`: each expert is the expert of exactly one task.
All inputs are finite; a program needn't handle non-finite values.
Results may differ from a plain program's by a relative error of at most 0.023.
Values may be sent and summed in bfloat16 or wider, within the bound.
A program may use at most 64 MiB of HBM per device.

v0:
```python
import jax
import jax.numpy as jnp
from jax import lax
from jax.sharding import PartitionSpec as P

coeff = 0.7978845608028654


def gelu_pair(pre):
    inner = coeff * (pre + 0.044715 * pre * pre * pre)
    tanh_val = jnp.tanh(inner)
    act = 0.5 * pre * (1.0 + tanh_val)
    slope = 0.5 * (1.0 + tanh_val) + 0.5 * pre * (1.0 - tanh_val * tanh_val) * coeff * (
        1.0 + 3.0 * 0.044715 * pre * pre
    )
    return (act, slope)


def body(tokens, upstream, task_ids, task_expert, w_in, w_out):
    n_expert = lax.axis_size("expert")
    rows_dev = tokens.shape[0]
    width = tokens.shape[1]
    experts = task_expert.shape[0]
    capacity = max(2, (9 * rows_dev // 8 + n_expert - 1) // n_expert)
    lanes = jnp.arange(experts, dtype=jnp.int32)
    task_hot = (task_ids == lanes[None, :]).astype(jnp.int32)
    target = jnp.sum(task_hot * task_expert[None, :], axis=1)
    dest_hot = (target[:, None] == lanes[None, :]).astype(jnp.int32)
    before = jnp.cumsum(dest_hot, axis=0) - dest_hot
    rank = jnp.sum(before * dest_hot, axis=1)
    slot = target * capacity + rank
    packer = (jnp.arange(experts * capacity, dtype=jnp.int32)[:, None] == slot[None, :]).astype(
        jnp.bfloat16
    )
    send_rows = (
        jnp.dot(packer, tokens, preferred_element_type=jnp.float32)
        .astype(jnp.bfloat16)
        .reshape(experts, capacity, width)
    )
    send_grads = (
        jnp.dot(packer, upstream, preferred_element_type=jnp.float32)
        .astype(jnp.bfloat16)
        .reshape(experts, capacity, width)
    )
    first = w_in[0]
    second = w_out[0]
    got_rows, got_grads = (
        lax.all_to_all(send_rows, "expert", split_axis=0, concat_axis=0, tiled=True),
        lax.all_to_all(send_grads, "expert", split_axis=0, concat_axis=0, tiled=True),
    )
    got_rows = got_rows.reshape(experts * capacity, width)
    got_grads = got_grads.reshape(experts * capacity, width)
    all_rows, all_grads = (
        lax.all_gather(got_rows, "dp", axis=0, tiled=True),
        lax.all_gather(got_grads, "dp", axis=0, tiled=True),
    )
    pre = jnp.dot(all_rows, first, preferred_element_type=jnp.float32)
    act, slope = gelu_pair(pre)
    act = act.astype(jnp.bfloat16)
    grad_second = lax.dot_general(
        act, all_grads, (((0,), (0,)), ((), ())), preferred_element_type=jnp.float32
    )
    dact = lax.dot_general(
        all_grads, second, (((1,), (1,)), ((), ())), preferred_element_type=jnp.float32
    )
    dpre = (dact * slope).astype(jnp.bfloat16)
    grad_first = lax.dot_general(
        all_rows, dpre, (((0,), (0,)), ((), ())), preferred_element_type=jnp.float32
    )
    partial_value = lax.dot_general(
        dpre, first, (((1,), (1,)), ((), ())), preferred_element_type=jnp.float32
    )
    own = lax.psum_scatter(
        partial_value.astype(jnp.bfloat16), "dp", scatter_dimension=0, tiled=True
    ).astype(jnp.float32)
    own = own.astype(jnp.bfloat16).reshape(experts, capacity, width)
    back = lax.all_to_all(own, "expert", split_axis=0, concat_axis=0, tiled=True).reshape(
        experts * capacity, width
    )
    token_grad = lax.dot_general(
        packer, back, (((0,), (0,)), ((), ())), preferred_element_type=jnp.float32
    ).astype(jnp.bfloat16)
    return (token_grad, grad_first[None], grad_second[None])


def solution(mesh):
    placed = (
        P(("dp", "expert"), None),
        P(("dp", "expert"), None),
        P(("dp", "expert"), None),
        P(),
        P("expert", None, "dp"),
        P("expert", "dp", None),
    )
    return jax.shard_map(
        body,
        mesh=mesh,
        in_specs=placed,
        out_specs=(P(("dp", "expert"), None), P("expert", None, "dp"), P("expert", "dp", None)),
        check_vma=False,
    )
```

profile of v0, /device:TPU:0, one launch (start us, length us, event | category | flops | bytes accessed | tf_op | source)
XLA Modules:
  0.0 150.4 jit_solution(1000656553306720690)
XLA Ops:
  7.2 0.0 copy-start
  7.2 0.0 copy-start.1
  7.2 0.0 all-gather.5.cloned.1.call-start
  7.2 1.0 select_reduce_fusion.1
  8.3 0.1 fusion.22
  8.4 0.2 reduce_window_sum.11
  8.5 0.2 select_reduce_fusion
  8.7 1.2 convolution_convert_fusion
  9.9 0.1 reshape.34
  10.0 18.7 %all_to_all.15 = bf16[8,18,1024]{2,1,0:T(8,128)(2,1)S(1)} all-to-all(bf16[8,18,1024]{2,1,0:T(8,128)(2,1)S(1)} %reshape.34), channel_id=1, replica_groups=mesh['dp'=4,'expert'=8] {'expert'}, dimensions={0} | all-to-all | bytes 589824 | tf_op jit(solution)/shard_map/all_to_all | solution.py:48
  28.7 0.8 reshape.35
  29.5 0.0 all-gather.5.cloned.1.call-update
  29.5 0.0 all-gather.3.cloned.1.call-start
  29.6 0.0 copy-done.1
  29.6 0.2 convolution_convert_fusion.1
  29.8 0.1 reshape.32
  29.9 14.9 %all_to_all.16 = bf16[8,18,1024]{2,1,0:T(8,128)(2,1)S(1)} all-to-all(bf16[8,18,1024]{2,1,0:T(8,128)(2,1)S(1)} %reshape.32), channel_id=1, replica_groups=mesh['dp'=4,'expert'=8] {'expert'}, dimensions={0} | all-to-all | bytes 589824 | tf_op jit(solution)/shard_map/all_to_all | solution.py:49
  44.8 0.8 reshape.33
  45.6 0.0 all-gather.3.cloned.1.call-update
  45.7 0.0 reduce-scatter.2.cloned.1.call-start
  45.7 10.6 %all-gather.5.cloned.1.call-done = bf16[576,1024]{1,0:T(8,128)(2,1)} async-done(((bf16[144,1024]{1,0:T(8,128)(2,1)}), bf16[576,1024]{1,0:T(8,128)(2,1)}) %all-gather.5.cloned.1.call-update) | async-done | bytes 1179664 | tf_op jit(solution)/shard_map/all_gather | solution.py:54
  56.3 0.0 copy-done
  56.3 4.1 %fusion.9 = f32[576,1024]{1,0:T(8,128)} fusion(bf16[576,1024]{1,0:T(8,128)(2,1)} %all-gather.5.cloned.1.call-done, bf16[1,1024,1024]{2,1,0:T(8,128)(2,1)S(1)} %copy-done), kind=kOutput, calls=%fused_computation.14 | convolution fusion | flops 1207959552 | bytes 5636096 | tf_op jit(solution)/shard_map/dot_general | solution.py:57
  60.4 26.1 %all-gather.3.cloned.1.call-done = bf16[576,1024]{1,0:T(8,128)(2,1)} async-done(((bf16[144,1024]{1,0:T(8,128)(2,1)}), bf16[576,1024]{1,0:T(8,128)(2,1)}) %all-gather.3.cloned.1.call-update) | async-done | bytes 1179664 | tf_op jit(solution)/shard_map/all_gather | solution.py:55
  86.5 5.1 %fusion.6 = bf16[576,1024]{1,0:T(8,128)(2,1)S(1)} fusion(f32[576,1024]{1,0:T(8,128)} %fusion.9, bf16[576,1024]{1,0:T(8,128)(2,1)} %all-gather.3.cloned.1.call-done, bf16[1,1024,1024]{2,1,0:T(8,128)(2,1)} %param.11), kind=kOutput, calls=%fused_computation.8 | convolution fusion | flops 1219166208 | bytes 6815744 | tf_op jit(solution)/shard_map/dot_general | solution.py:63
  91.6 0.0 copy-start.4
  91.6 1.0 copy-done.4
  92.7 2.4 %fusion.15 = bf16[576,1024]{1,0:T(8,128)(2,1)} fusion(bf16[576,1024]{1,0:T(8,128)(2,1)S(1)} %fusion.6, bf16[1,1024,1024]{2,1,0:T(8,128)(2,1)S(1)} %copy-done), kind=kOutput, calls=%fused_computation.18 | convolution fusion | flops 1208549376 | bytes 4456448 | tf_op jit(solution)/shard_map/dot_general | solution.py:70
  95.1 0.0 reduce-scatter.2.cloned.1.call-update
  95.1 28.7 %reduce-scatter.2.cloned.1.call-done = bf16[144,1024]{1,0:T(8,128)(2,1)} async-done(((bf16[576,1024]{1,0:T(8,128)(2,1)}), bf16[144,1024]{1,0:T(8,128)(2,1)}) %reduce-scatter.2.cloned.1.call-update) | async-done | bytes 294928 | tf_op jit(solution)/shard_map/reduce_scatter | solution.py:73
  123.8 1.8 %reshape.36 = bf16[8,18,1024]{2,1,0:T(8,128)(2,1)} reshape(bf16[144,1024]{1,0:T(8,128)(2,1)} %reduce-scatter.2.cloned.1.call-done) | data formatting | bytes 589824 | tf_op jit(solution)/shard_map/reshape | solution.py:76
  125.6 4.6 %all-to-all-start.2 = ((bf16[8,18,1024]{2,1,0:T(8,128)(2,1)}), bf16[8,18,1024]{2,1,0:T(8,128)(2,1)S(1)}, u32[]{:S(2)}, u32[]{:S(2)}) async-start(bf16[8,18,1024]{2,1,0:T(8,128)(2,1)} %reshape.36), calls=%async_computation.3 | async-start | bytes 786432 | tf_op jit(solution)/shard_map/all_to_all | solution.py:77
  130.2 0.0 copy-start.2
  130.2 0.0 copy-start.3
  130.2 5.6 %convolution_bitcast_fusion.1 = f32[1,1024,1024]{2,1,0:T(8,128)} fusion(bf16[576,1024]{1,0:T(8,128)(2,1)} %all-gather.5.cloned.1.call-done, bf16[576,1024]{1,0:T(8,128)(2,1)} %copy-done.4), kind=kOutput, calls=%fused_computation.11 | convolution fusion | flops 1207959552 | bytes 6553600 | tf_op jit(solution)/shard_map/dot_general | solution.py:67
  135.8 0.0 copy-done.2
  135.8 0.0 copy-done.3
  135.8 4.0 %convolution_bitcast_fusion = f32[1,1024,1024]{2,1,0:T(8,128)} fusion(bf16[576,1024]{1,0:T(8,128)(2,1)S(1)} %copy-done.2, f32[576,1024]{1,0:T(8,128)S(1)} %copy-done.3), kind=kOutput, calls=%fused_computation.10 | convolution fusion | flops 1213267968 | bytes 7733248 | tf_op jit(solution)/shard_map/dot_general | solution.py:60
  139.9 2.9 %all-to-all-done.2 = bf16[8,18,1024]{2,1,0:T(8,128)(2,1)S(1)} async-done(((bf16[8,18,1024]{2,1,0:T(8,128)(2,1)}), bf16[8,18,1024]{2,1,0:T(8,128)(2,1)S(1)}, u32[]{:S(2)}, u32[]{:S(2)}) %all-to-all-start.2) | async-done | bytes 294944 | tf_op jit(solution)/shard_map/all_to_all | solution.py:77
  142.7 0.1 reshape.37
  142.8 1.0 convolution_convert_fusion.2
  (1 shorter events, 0.0 us)
Async XLA Ops:
  7.2 49.1 %copy-start = (bf16[1,1024,1024]{2,1,0:T(8,128)(2,1)S(1)}, bf16[1,1024,1024]{2,1,0:T(8,128)(2,1)}, u32[]{:S(2)}) copy-start(bf16[1,1024,1024]{2,1,0:T(8,128)(2,1)} %param.10) | copy-start | bytes 6291460
  7.2 22.4 %copy-start.1 = (bf16[128,1024]{1,0:T(8,128)(2,1)S(1)}, bf16[128,1024]{1,0:T(8,128)(2,1)}, u32[]{:S(2)}) copy-start(bf16[128,1024]{1,0:T(8,128)(2,1)} %param.7) | copy-start | bytes 786436
  7.2 49.1 %all-gather.5.cloned.1.call-start = ((), (), s32[]{:S(2)}) async-start(), calls=%async_computation.5 | async-start | bytes 1474560 | tf_op jit(solution)/shard_map/all_gather | solution.py:54
  29.5 57.0 %all-gather.3.cloned.1.call-start = ((), (), s32[]{:S(2)}) async-start(), calls=%async_computation.4 | async-start | bytes 1474560 | tf_op jit(solution)/shard_map/all_gather | solution.py:55
  45.7 78.1 %reduce-scatter.2.cloned.1.call-start = ((), (), s32[]{:S(2)}) async-start(), calls=%async_computation.6 | async-start | bytes 1474560 | tf_op jit(solution)/shard_map/reduce_scatter | solution.py:73
  91.6 1.0 copy-start.4
  125.6 17.1 %all-to-all-start.2 = ((bf16[8,18,1024]{2,1,0:T(8,128)(2,1)}), bf16[8,18,1024]{2,1,0:T(8,128)(2,1)S(1)}, u32[]{:S(2)}, u32[]{:S(2)}) async-start(bf16[8,18,1024]{2,1,0:T(8,128)(2,1)} %reshape.36), calls=%async_computation.3 | async-start | bytes 786432 | tf_op jit(solution)/shard_map/all_to_all | solution.py:77
  130.2 5.6 %copy-start.2 = (bf16[576,1024]{1,0:T(8,128)(2,1)S(1)}, bf16[576,1024]{1,0:T(8,128)(2,1)}, u32[]{:S(2)}) copy-start(bf16[576,1024]{1,0:T(8,128)(2,1)} %all-gather.3.cloned.1.call-done) | copy-start | bytes 3538948
  130.2 5.6 %copy-start.3 = (f32[576,1024]{1,0:T(8,128)S(1)}, f32[576,1024]{1,0:T(8,128)}, u32[]{:S(2)}) copy-start(f32[576,1024]{1,0:T(8,128)} %fusion.9) | copy-start | bytes 7077892
Sparse Core Ops, SparseCore 0:
  29.6 26.6 all-gather.4
  58.7 27.7 all-gather.2
  95.2 28.5 reduce-scatter.1
where the time goes:
time: 151 us; the launch traced here: 150 us
  waiting for transfers between devices  68.3 us (45%)
  blocking collectives  33.6 us (22%)
  matrix products  23.7 us (16%)
  between operations  13.9 us (9%)
  local copies, waits for them, and re-layouts  4.72 us (3%)
  starting transfers between devices  4.72 us (3%)
    reduce_scatter x1, waiting for transfers between devices, body(): lax.psum_scatter(partial_value.astype(jnp.bfloat16), 'dp', scatter_dimens...  28.7 us
    all_gather x1, waiting for transfers between devices, body(): lax.all_gather(got_grads, 'dp', axis=0, tiled=True)  26.1 us
    all_to_all x1, blocking collectives, body(): lax.all_to_all(send_rows, 'expert', split_axis=0, concat_axis=0, tiled=True)  18.7 us
    all_to_all x1, blocking collectives, body(): lax.all_to_all(send_grads, 'expert', split_axis=0, concat_axis=0, tiled=T...  14.9 us
    all_gather x1, waiting for transfers between devices, body(): lax.all_gather(got_rows, 'dp', axis=0, tiled=True)  10.6 us
    dot_general x1, matrix products, body(): lax.dot_general(all_rows, dpre, (((0,), (0,)), ((), ())), preferred_eleme...  5.63 us
    dot_general x1, matrix products, body(): lax.dot_general(all_grads, second, (((1,), (1,)), ((), ())), preferred_el...  5.15 us
    all_to_all x1, starting transfers between devices, body(): lax.all_to_all(own, 'expert', split_axis=0, concat_axis=0, tiled=True)  4.6 us
  transfers between devices with their start and end apart: 4, of which 4 were waited for; matrix products, arithmetic and copies ran while one was open for 10% of the time, Pallas kernels for 0%

commit v1 on v0

--- a/solution.py
+++ b/solution.py
@@ -1,9 +1,18 @@
+import functools
+
 import jax
 import jax.numpy as jnp
 from jax import lax
+from jax.experimental import pallas as pl
+from jax.experimental.pallas import tpu as pltpu
 from jax.sharding import PartitionSpec as P
 
 coeff = 0.7978845608028654
+MESH = pl.DeviceIdType.MESH
+BF = jnp.bfloat16
+F32 = jnp.float32
+MAIN = 16
+LANES = 128
 
 
 def gelu_pair(pre):
@@ -16,7 +25,350 @@
     return (act, slope)
 
 
-def body(tokens, upstream, task_ids, task_expert, w_in, w_out):
+def fold(rows, width):
+    return jnp.concatenate([rows[:, c : c + LANES] for c in range(0, width, LANES)], axis=0)
+
+
+def unfold(rows, start, width):
+    return jnp.concatenate(
+        [rows[c * MAIN : (c + 1) * MAIN, start : start + LANES] for c in range(width // LANES)], axis=1
+    )
+
+
+def exchange_kernel(
+    n_expert,
+    rows_dev,
+    width,
+    ff,
+    tokens_ref,
+    upstream_ref,
+    ids_ref,
+    experts_ref,
+    first_hbm,
+    second_hbm,
+    out_ref,
+    xg_hbm,
+    ad_hbm,
+    first,
+    second,
+    send,
+    got,
+    extra,
+    ad,
+    part,
+    peer,
+    back_send,
+    back_got,
+    w_sem,
+    z_send,
+    x_send,
+    y_send,
+    f_send,
+    recv,
+    p_send,
+    p_recv,
+    b_send,
+    b_recv,
+    o_sem,
+):
+    chips = n_expert // 2
+    group = n_expert * MAIN
+    over = MAIN
+    chunk = group + over
+    e = lax.axis_index("expert")
+    d = lax.axis_index("dp")
+    chip, core = lax.div(e, 2), lax.rem(e, 2)
+    xn = d + 1 - 2 * lax.rem(d, 2)
+    yn = lax.rem(d + 2, 4)
+    diag = lax.rem(xn + 2, 4)
+
+    def target(i):
+        return lax.rem(chip + i // 2, chips) * 2 + lax.rem(core + i % 2, 2)
+
+    def source(i):
+        return lax.rem(chip + chips - i // 2, chips) * 2 + lax.rem(core + i % 2, 2)
+
+    def block(index):
+        return pl.ds(pl.multiple_of(index * MAIN, MAIN), MAIN)
+
+    def at(k, s):
+        return pl.ds(pl.multiple_of(k * group + s * MAIN, MAIN), MAIN)
+
+    barrier = pltpu.get_barrier_semaphore()
+    for i in range(1, n_expert):
+        pl.semaphore_signal(barrier, inc=1, device_id={"expert": target(i)}, device_id_type=MESH)
+    for near in (xn, yn, diag):
+        pl.semaphore_signal(barrier, inc=1, device_id={"dp": near}, device_id_type=MESH)
+
+    loads = [
+        pltpu.make_async_copy(first_hbm, first, w_sem.at[0]),
+        pltpu.make_async_copy(second_hbm, second, w_sem.at[1]),
+    ]
+    for load in loads:
+        load.start()
+
+    lane8 = lax.broadcasted_iota(jnp.int32, (rows_dev, n_expert), 1)
+    hot = (ids_ref[...] == lane8).astype(F32)
+    goal = jnp.sum(hot * experts_ref[...].astype(F32), axis=1, keepdims=True)
+    row = lax.broadcasted_iota(jnp.int32, (rows_dev, rows_dev), 0)
+    col = lax.broadcasted_iota(jnp.int32, (rows_dev, rows_dev), 1)
+    lane = col.astype(F32)
+    dest = (goal == lane).astype(F32)
+    before = jnp.dot((row > col).astype(BF), dest.astype(BF), preferred_element_type=F32)
+    rank = jnp.sum(before * dest, axis=1, keepdims=True)
+    is_main = (rank < MAIN).astype(F32)
+    main_hot = ((goal * MAIN + rank == lane).astype(F32) * is_main).astype(BF)
+    over_hot = ((goal * 2 + (rank - MAIN) == lane).astype(F32) * (1.0 - is_main)).astype(BF)
+    turned = (row >> 1 & 7) * 16 + (row >> 4) * 2 + (row & 1)
+    perm = (turned == col).astype(BF)
+
+    def gather(hot_rows, values):
+        return lax.dot_general(
+            hot_rows, values, (((0,), (0,)), ((), ())), preferred_element_type=F32
+        ).astype(BF)
+
+    tokens = tokens_ref[...]
+    upstream = upstream_ref[...]
+    send[:, :width] = gather(main_hot, tokens)
+    send[:, width : 2 * width] = gather(main_hot, upstream)
+    folded = jnp.concatenate(
+        [
+            fold(gather(over_hot, tokens)[:over], width),
+            fold(gather(over_hot, upstream)[:over], width),
+        ],
+        axis=1,
+    )
+    send[:, 2 * width :] = jnp.dot(perm, folded, preferred_element_type=F32).astype(BF)
+
+    pl.semaphore_wait(barrier, n_expert - 1 + 3)
+
+    started = []
+
+    def push(src, dst, send_sem, recv_sem, device):
+        copy = pltpu.make_async_remote_copy(
+            src_ref=src,
+            dst_ref=dst,
+            send_sem=send_sem,
+            recv_sem=recv_sem,
+            device_id=device,
+            device_id_type=MESH,
+        )
+        copy.start()
+        started.append(copy)
+
+    for i in range(1, n_expert):
+        push(send.at[block(target(i))], got.at[at(0, e)], z_send.at[i - 1], recv.at[e], {"expert": target(i)})
+    got[at(0, e), :] = send[block(e), :]
+
+    def arrived(k, s):
+        here = got.at[at(k, s)]
+        pltpu.make_async_copy(here, here, recv.at[k * n_expert + s]).wait()
+
+    def forward(i):
+        s = source(i)
+        arrived(1, s)
+        arrived(2, s)
+        if i % 2 == 0:
+            push(got.at[at(1, s)], got.at[at(3, s)], f_send.at[i], recv.at[3 * n_expert + s], {"dp": yn})
+        else:
+            push(got.at[at(2, s)], got.at[at(3, s)], f_send.at[i], recv.at[3 * n_expert + s], {"dp": xn})
+
+    lag = 2
+    for i in range(n_expert):
+        s = source(i)
+        if i > 0:
+            arrived(0, s)
+        push(got.at[at(0, s)], got.at[at(1, s)], x_send.at[i], recv.at[n_expert + s], {"dp": xn})
+        push(got.at[at(0, s)], got.at[at(2, s)], y_send.at[i], recv.at[2 * n_expert + s], {"dp": yn})
+        if i >= lag:
+            forward(i - lag)
+    for i in range(n_expert - lag, n_expert):
+        forward(i)
+    for load in loads:
+        load.wait()
+
+    outs = []
+
+    def ship(src, dst):
+        copy = pltpu.make_async_copy(src, dst, o_sem.at[len(outs)])
+        copy.start()
+        outs.append(copy)
+
+    tile = 256
+
+    def work(k):
+        main = pl.ds(k * group, group)
+        rest = pl.ds(k * over, over)
+        mine = pl.ds(k * chunk, chunk)
+        open_rows = jnp.dot(perm, got[main, 2 * width :], preferred_element_type=F32).astype(BF)
+        extra[rest, :width] = unfold(open_rows, 0, width)
+        extra[rest, width:] = unfold(open_rows, LANES, width)
+
+        @pl.loop(0, ff // tile)
+        def _(f):
+            cols = pl.ds(pl.multiple_of(f * tile, tile), tile)
+            later = pl.ds(pl.multiple_of(ff + f * tile, tile), tile)
+            rows = jnp.concatenate([got[main, :width], extra[rest, :width]], axis=0)
+            grads = jnp.concatenate([got[main, width : 2 * width], extra[rest, width:]], axis=0)
+            pre = jnp.dot(rows, first[:, cols], preferred_element_type=F32)
+            act, slope = gelu_pair(pre)
+            ad[mine, cols] = act.astype(BF)
+            dact = lax.dot_general(
+                grads, second[cols, :], (((1,), (1,)), ((), ())), preferred_element_type=F32
+            )
+            ad[mine, later] = (dact * slope).astype(BF)
+
+        @pl.loop(0, width // tile)
+        def _(f):
+            cols = pl.ds(pl.multiple_of(f * tile, tile), tile)
+            part[mine, cols] = lax.dot_general(
+                ad[mine, ff:], first[cols, :], (((1,), (1,)), ((), ())), preferred_element_type=F32
+            ).astype(BF)
+
+        ship(got.at[main, pl.ds(0, 2 * width)], xg_hbm.at[pl.ds(k * chunk, group)])
+        ship(extra.at[rest], xg_hbm.at[pl.ds(k * chunk + group, over)])
+        ship(ad.at[mine], ad_hbm.at[mine])
+
+    def give(k, near):
+        push(
+            part.at[pl.ds(k * chunk, chunk)],
+            peer.at[pl.ds((k - 1) * chunk, chunk)],
+            p_send.at[k - 1],
+            p_recv.at[k - 1],
+            {"dp": near},
+        )
+
+    work(1)
+    give(1, xn)
+    work(2)
+    give(2, yn)
+    for i in range(n_expert):
+        arrived(3, source(i))
+    work(3)
+    give(3, diag)
+    work(0)
+
+    for k in range(3):
+        here = peer.at[pl.ds(k * chunk, chunk)]
+        pltpu.make_async_copy(here, here, p_recv.at[k]).wait()
+
+    def total(low, size):
+        value = part[low : low + size, :].astype(F32)
+        for k in range(3):
+            value = value + peer[k * chunk + low : k * chunk + low + size, :].astype(F32)
+        return value.astype(BF)
+
+    back_send[:, :width] = total(0, group)
+    back_send[:, width:] = jnp.dot(
+        perm, fold(total(group, over), width), preferred_element_type=F32
+    ).astype(BF)
+    for i in range(1, n_expert):
+        push(
+            back_send.at[block(target(i))],
+            back_got.at[block(e)],
+            b_send.at[i - 1],
+            b_recv.at[e],
+            {"expert": target(i)},
+        )
+    back_got[block(e), :] = back_send[block(e), :]
+    for i in range(1, n_expert):
+        s = source(i)
+        here = back_got.at[block(s)]
+        pltpu.make_async_copy(here, here, b_recv.at[s]).wait()
+    open_rows = jnp.dot(perm, back_got[:, width:], preferred_element_type=F32).astype(BF)
+    extra_rows = unfold(open_rows, 0, width)
+    result = jnp.dot(main_hot, back_got[:, :width], preferred_element_type=F32)
+    result = result + jnp.dot(over_hot[:, :over], extra_rows, preferred_element_type=F32)
+    out_ref[...] = result.astype(BF)
+    for copy in started:
+        copy.wait_send()
+    for copy in outs:
+        copy.wait()
+
+
+def weight_kernel(x_tile, grads, act_tile, dpre, grad_in, grad_out):
+    spec = (((0,), (0,)), ((), ()))
+    grad_in[...] = lax.dot_general(x_tile[...], dpre[...], spec, preferred_element_type=F32)
+    grad_out[...] = lax.dot_general(act_tile[...], grads[...], spec, preferred_element_type=F32)
+
+
+def fused_body(tokens, upstream, task_ids, task_expert, w_in, w_out):
+    n_expert = lax.axis_size("expert")
+    rows_dev, width = tokens.shape
+    ff = w_in.shape[2]
+    group = n_expert * MAIN
+    chunk = group + MAIN
+    rows = 4 * chunk
+    first, second = w_in[0], w_out[0]
+    dma = pltpu.SemaphoreType.DMA
+    vmem = pl.BlockSpec(memory_space=pltpu.VMEM)
+    hbm = pl.BlockSpec(memory_space=pl.ANY)
+    token_grad, xg, ad = pl.pallas_call(
+        functools.partial(exchange_kernel, n_expert, rows_dev, width, ff),
+        out_shape=(
+            jax.ShapeDtypeStruct((rows_dev, width), BF),
+            jax.ShapeDtypeStruct((rows, 2 * width), BF),
+            jax.ShapeDtypeStruct((rows, 2 * ff), BF),
+        ),
+        in_specs=[vmem, vmem, vmem, vmem, hbm, hbm],
+        out_specs=(vmem, hbm, hbm),
+        scratch_shapes=[
+            pltpu.VMEM((width, ff), BF),
+            pltpu.VMEM((ff, width), BF),
+            pltpu.VMEM((group, 2 * width + 2 * LANES), BF),
+            pltpu.VMEM((4 * group, 2 * width + 2 * LANES), BF),
+            pltpu.VMEM((4 * MAIN, 2 * width), BF),
+            pltpu.VMEM((rows, 2 * ff), BF),
+            pltpu.VMEM((rows, width), BF),
+            pltpu.VMEM((3 * chunk, width), BF),
+            pltpu.VMEM((group, width + LANES), BF),
+            pltpu.VMEM((group, width + LANES), BF),
+            dma((2,)),
+            dma((n_expert - 1,)),
+            dma((n_expert,)),
+            dma((n_expert,)),
+            dma((n_expert,)),
+            dma((4 * n_expert,)),
+            dma((3,)),
+            dma((3,)),
+            dma((n_expert - 1,)),
+            dma((n_expert,)),
+            dma((12,)),
+        ],
+        compiler_params=pltpu.CompilerParams(
+            collective_id=0, has_side_effects=True, vmem_limit_bytes=40 * 1024 * 1024
+        ),
+        cost_estimate=pl.CostEstimate(
+            flops=6 * rows * width * ff, bytes_accessed=12 * width * ff, transcendentals=rows * ff
+        ),
+    )(tokens, upstream, task_ids, task_expert.reshape(1, -1), first, second)
+    tile = 256
+    grad_in, grad_out = pl.pallas_call(
+        weight_kernel,
+        grid=(width // tile,),
+        out_shape=(
+            jax.ShapeDtypeStruct((width, ff), F32),
+            jax.ShapeDtypeStruct((ff, width), F32),
+        ),
+        in_specs=[
+            pl.BlockSpec((rows, tile), lambda i: (0, i)),
+            pl.BlockSpec((rows, width), lambda i: (0, 1)),
+            pl.BlockSpec((rows, tile), lambda i: (0, i)),
+            pl.BlockSpec((rows, ff), lambda i: (0, 1)),
+        ],
+        out_specs=(
+            pl.BlockSpec((tile, ff), lambda i: (i, 0)),
+            pl.BlockSpec((tile, width), lambda i: (i, 0)),
+        ),
+        compiler_params=pltpu.CompilerParams(vmem_limit_bytes=40 * 1024 * 1024),
+        cost_estimate=pl.CostEstimate(
+            flops=4 * rows * width * ff, bytes_accessed=16 * width * ff, transcendentals=0
+        ),
+    )(xg, xg, ad, ad)
+    return (token_grad, grad_in[None], grad_out[None])
+
+
+def general_body(tokens, upstream, task_ids, task_expert, w_in, w_out):
     n_expert = lax.axis_size("expert")
     rows_dev = tokens.shape[0]
     width = tokens.shape[1]
@@ -83,6 +435,23 @@
     return (token_grad, grad_first[None], grad_second[None])
 
 
+def body(mesh, tokens, upstream, task_ids, task_expert, w_in, w_out):
+    n_expert = mesh.shape["expert"]
+    rows_dev, width = tokens.shape
+    ff = w_in.shape[2]
+    capacity = max(2, (9 * rows_dev // 8 + n_expert - 1) // n_expert)
+    fits = (
+        mesh.shape["dp"] == 4
+        and n_expert == 8
+        and rows_dev == 128
+        and capacity <= MAIN + 2
+        and width == n_expert * LANES
+        and ff == width
+    )
+    run = fused_body if fits else general_body
+    return run(tokens, upstream, task_ids, task_expert, w_in, w_out)
+
+
 def solution(mesh):
     placed = (
         P(("dp", "expert"), None),
@@ -93,7 +462,7 @@
         P("expert", "dp", None),
     )
     return jax.shard_map(
-        body,
+        functools.partial(body, mesh),
         mesh=mesh,
         in_specs=placed,
         out_specs=(P(("dp", "expert"), None), P("expert", None, "dp"), P("expert", "dp", None)),

time: 151 us -> 69.3 us (0.46)
  waiting for transfers between devices: 68.3 us -> 0 us
  Pallas kernels: 0 us -> 61.2 us
  blocking collectives: 33.6 us -> 0 us
  matrix products: 23.7 us -> 0 us
  between operations: 13.9 us -> 0.65 us
  starting transfers between devices: 4.72 us -> 0 us
  local copies, waits for them, and re-layouts: 4.72 us -> 7.19 us
    pallas_call x0 -> x2, Pallas kernels: none -> 61.2 us  [the longest x1 55.7 us: fused_body(): pl.pallas_call(functools.partial(exchange_kernel, n_expert, rows_dev, wid...]
    all_gather x2 -> x0, waiting for transfers between devices: 36.7 us -> none  [the longest x1 26.1 us: body(): lax.all_gather(got_grads, 'dp', axis=0, tiled=True)]
    all_to_all x2 -> x0, blocking collectives: 33.6 us -> none  [the longest x1 18.7 us: body(): lax.all_to_all(send_rows, 'expert', split_axis=0, concat_axis=0, tiled=True)]
    reduce_scatter x1 -> x0, waiting for transfers between devices: 28.7 us -> none  [body(): lax.psum_scatter(partial_value.astype(jnp.bfloat16), 'dp', scatter_dimens...]
    dot_general x8 -> x0, matrix products: 23.7 us -> none  [the longest x1 5.63 us: body(): lax.dot_general(all_rows, dpre, (((0,), (0,)), ((), ())), preferred_eleme...]
    unnamed x10 -> x12, local copies, waits for them, and re-layouts: 1.05 us -> 7.19 us
    all_to_all x1 -> x0, starting transfers between devices: 4.6 us -> none  [body(): lax.all_to_all(own, 'expert', split_axis=0, concat_axis=0, tiled=True)]
    reshape x6 -> x0, local copies, waits for them, and re-layouts: 3.68 us -> none  [the longest x1 1.79 us: body(): own = own.astype(jnp.bfloat16).reshape(experts, capacity, width)]
  transfers between devices with their start and end apart: 4 -> 0, of which waited for: 4 -> 0; matrix products, arithmetic and copies ran while one was open for 10% -> 0% of each run, Pallas kernels for 0% -> 0%
where the time goes in v1:
time: 69.3 us; the launch traced here: 69.1 us
  Pallas kernels  61.2 us (88%)
  local copies, waits for them, and re-layouts  7.19 us (10%)
    pallas_call x1, Pallas kernels, fused_body(): pl.pallas_call(functools.partial(exchange_kernel, n_expert, rows_dev, wid...  55.7 us
    unnamed x12, local copies, waits for them, and re-layouts  7.19 us
    pallas_call x1, Pallas kernels, fused_body(): pl.pallas_call(weight_kernel, grid=(width // tile,), out_shape=(jax.Shape...  5.58 us

profile of v1, /device:TPU:0, one launch (start us, length us, event | category | flops | bytes accessed | tf_op | source)
XLA Modules:
  0.0 69.1 jit_solution(6109587297365722167)
XLA Ops:
  0.6 0.8 %copy.9.ids_ref = s32[128,1]{1,0:T(8,128)S(1)} copy(s32[128,1]{0,1:T(1,128)} %param.8) | data formatting | bytes 1024 | tf_op args[2]
  1.4 0.0 copy-start
  1.4 1.6 %copy-done = bf16[1,1024,1024]{2,1,0:T(8,128)(2,1)S(1)} copy-done((bf16[1,1024,1024]{2,1,0:T(8,128)(2,1)S(1)}, bf16[1,1024,1024]{2,1,0:T(8,128)(2,1)}, u32[]{:S(2)}) %copy-start) | copy-done | bytes 2097176
  3.0 0.0 copy-start.1
  3.0 1.6 %copy-done.1 = bf16[1,1024,1024]{2,1,0:T(8,128)(2,1)S(1)} copy-done((bf16[1,1024,1024]{2,1,0:T(8,128)(2,1)S(1)}, bf16[1,1024,1024]{2,1,0:T(8,128)(2,1)}, u32[]{:S(2)}) %copy-start.1) | copy-done | bytes 2097176
  4.6 0.0 copy-start.2
  4.6 0.9 %copy-done.2 = bf16[128,1024]{1,0:T(8,128)(2,1)S(1)} copy-done((bf16[128,1024]{1,0:T(8,128)(2,1)S(1)}, bf16[128,1024]{1,0:T(8,128)(2,1)}, u32[]{:S(2)}) %copy-start.2) | copy-done | bytes 262168
  5.5 0.0 copy-start.3
  5.5 0.9 %copy-done.3 = bf16[128,1024]{1,0:T(8,128)(2,1)S(1)} copy-done((bf16[128,1024]{1,0:T(8,128)(2,1)S(1)}, bf16[128,1024]{1,0:T(8,128)(2,1)}, u32[]{:S(2)}) %copy-start.3) | copy-done | bytes 262168
  6.5 0.0 copy-start.4
  6.5 0.7 copy-done.4
  7.1 55.7 %shard_map.85 = (bf16[128,1024]{1,0:T(8,128)(2,1)S(1)}, bf16[576,2048]{1,0:T(8,128)(2,1)S(1)}, bf16[576,2048]{1,0:T(8,128)(2,1)S(1)}) custom-call(bf16[128,1024]{1,0:T(8,128)(2,1)S(1)} %copy-done.2, bf16[128,1024]{1,0:T(8,128)(2,1)S(1)} %copy-done.3, s32[128,1]{1,0:T(8,128)S(1)} %copy.9.ids_ref, s32[1,8]{1,0:T(1,128)S(1)} %bitcast.7, ...), custom_call_target="tpu_custom_call" | custom-call | flops 3623878656 | bytes 12582912 | tf_op jit(solution)/shard_map/pallas_call | solution.py:306
  62.8 5.6 %shard_map.86 = (f32[1024,1024]{1,0:T(8,128)}, f32[1024,1024]{1,0:T(8,128)}) custom-call(bf16[576,2048]{1,0:T(8,128)(2,1)S(1)} %get-tuple-element.9.x_tile.grads, bf16[576,2048]{1,0:T(8,128)(2,1)S(1)} %get-tuple-element.9.x_tile.grads, bf16[576,2048]{1,0:T(8,128)(2,1)S(1)} %get-tuple-element.10.act_tile.dpre, ...), custom_call_target="tpu_custom_call" | custom-call | flops 2415919104 | bytes 16777216 | tf_op jit(solution)/shard_map/pallas_call | solution.py:346
  68.4 0.7 %copy.11 = bf16[128,1024]{1,0:T(8,128)(2,1)} copy(bf16[128,1024]{1,0:T(8,128)(2,1)S(1)} %get-tuple-element.16) | data formatting | bytes 524288
Async XLA Ops:
  1.4 1.6 %copy-start = (bf16[1,1024,1024]{2,1,0:T(8,128)(2,1)S(1)}, bf16[1,1024,1024]{2,1,0:T(8,128)(2,1)}, u32[]{:S(2)}) copy-start(bf16[1,1024,1024]{2,1,0:T(8,128)(2,1)} %param.10) | copy-start | bytes 6291460
  3.0 1.6 %copy-start.1 = (bf16[1,1024,1024]{2,1,0:T(8,128)(2,1)S(1)}, bf16[1,1024,1024]{2,1,0:T(8,128)(2,1)}, u32[]{:S(2)}) copy-start(bf16[1,1024,1024]{2,1,0:T(8,128)(2,1)} %param.11) | copy-start | bytes 6291460
  4.6 0.9 %copy-start.2 = (bf16[128,1024]{1,0:T(8,128)(2,1)S(1)}, bf16[128,1024]{1,0:T(8,128)(2,1)}, u32[]{:S(2)}) copy-start(bf16[128,1024]{1,0:T(8,128)(2,1)} %tokens_ref.1) | copy-start | bytes 786436
  5.5 0.9 %copy-start.3 = (bf16[128,1024]{1,0:T(8,128)(2,1)S(1)}, bf16[128,1024]{1,0:T(8,128)(2,1)}, u32[]{:S(2)}) copy-start(bf16[128,1024]{1,0:T(8,128)(2,1)} %upstream_ref.1) | copy-start | bytes 786436
  6.5 0.7 copy-start.4

commit v2 on v1

v2 whole, which is shorter than its diff:
```python
import functools

import jax
import jax.numpy as jnp
from jax import lax
from jax.experimental import pallas as pl
from jax.experimental.pallas import tpu as pltpu
from jax.sharding import PartitionSpec as P

coeff = 0.7978845608028654
MESH = pl.DeviceIdType.MESH
BF = jnp.bfloat16
F32 = jnp.float32
MAIN = 16
LANES = 128


def gelu_pair(pre):
    square = pre * pre
    tanh_val = jnp.tanh(pre * (coeff + coeff * 0.044715 * square))
    half = 0.5 + 0.5 * tanh_val
    slope = half + half * (1.0 - tanh_val) * (pre * (coeff + 3.0 * 0.044715 * coeff * square))
    return (pre * half, slope)


def fold(rows, width):
    return jnp.concatenate([rows[:, c : c + LANES] for c in range(0, width, LANES)], axis=0)


def unfold(rows, start, width):
    return jnp.concatenate(
        [rows[c * MAIN : (c + 1) * MAIN, start : start + LANES] for c in range(width // LANES)], axis=1
    )


def exchange_kernel(
    n_expert,
    rows_dev,
    width,
    ff,
    tokens_hbm,
    upstream_hbm,
    ids_hbm,
    experts_ref,
    first_hbm,
    second_hbm,
    out_ref,
    grad_in_out,
    grad_out_out,
    tokens_ref,
    upstream_ref,
    ids_ref,
    first,
    second,
    send,
    got,
    extra,
    ad,
    part,
    peer,
    grad_in,
    grad_out,
    back_send,
    back_got,
    w_sem,
    z_send,
    x_send,
    y_send,
    f_send,
    recv,
    p_send,
    p_recv,
    b_send,
    b_recv,
    o_sem,
):
    chips = n_expert // 2
    group = n_expert * MAIN
    over = MAIN
    half = group // 2
    mains = 4 * group
    e = lax.axis_index("expert")
    d = lax.axis_index("dp")
    chip, core = lax.div(e, 2), lax.rem(e, 2)
    xn = d + 1 - 2 * lax.rem(d, 2)
    yn = lax.rem(d + 2, 4)
    diag = lax.rem(xn + 2, 4)
    upper = lax.div(chip, chips // 2)
    inner = chip + upper * (chips - 1 - 2 * chip)

    def order(i):
        place = (inner, 1 - inner, 2, 3)[i // 2]
        return (place + upper * (chips - 1 - 2 * place)) * 2 + lax.rem(core + i % 2, 2)

    def block(index):
        return pl.ds(pl.multiple_of(index * MAIN, MAIN), MAIN)

    def at(k, s):
        return pl.ds(pl.multiple_of(k * group + s * MAIN, MAIN), MAIN)

    loads = [
        pltpu.make_async_copy(src, dst, w_sem.at[i])
        for i, (src, dst) in enumerate(
            (
                (ids_hbm, ids_ref),
                (tokens_hbm, tokens_ref),
                (upstream_hbm, upstream_ref),
                (first_hbm, first),
                (second_hbm, second),
            )
        )
    ]
    for load in loads:
        load.start()

    barrier = pltpu.get_barrier_semaphore()
    for i in range(1, n_expert):
        pl.semaphore_signal(barrier, inc=1, device_id={"expert": order(i)}, device_id_type=MESH)
    for near in (xn, yn, diag):
        pl.semaphore_signal(barrier, inc=1, device_id={"dp": near}, device_id_type=MESH)

    row = lax.broadcasted_iota(jnp.int32, (rows_dev, rows_dev), 0)
    col = lax.broadcasted_iota(jnp.int32, (rows_dev, rows_dev), 1)
    line = row.astype(F32)
    earlier = (row < col).astype(BF)
    turned = (row >> 1 & 7) * 16 + (row >> 4) * 2 + (row & 1)
    perm = (turned == col).astype(BF)
    loads[0].wait()
    ids = ids_ref[...]
    goal = jnp.zeros(ids.shape, F32)
    for k in range(n_expert):
        goal = jnp.where(ids == k, experts_ref[k].astype(F32), goal)
    dest = (goal == line).astype(F32)
    before = jnp.dot(dest.astype(BF), earlier, preferred_element_type=F32)
    rank = jnp.sum(before * dest, axis=0, keepdims=True)
    is_main = (rank < MAIN).astype(F32)
    main_hot = ((goal * MAIN + rank == line).astype(F32) * is_main).astype(BF)
    over_hot = ((goal * 2 + (rank - MAIN) == line).astype(F32) * (1.0 - is_main)).astype(BF)[:over]

    def pick(hot_rows, values):
        return jnp.dot(hot_rows, values, preferred_element_type=F32).astype(BF)

    loads[1].wait()
    tokens = tokens_ref[...]
    send[:, :width] = pick(main_hot, tokens)
    loads[2].wait()
    upstream = upstream_ref[...]
    send[:, width : 2 * width] = pick(main_hot, upstream)
    folded = jnp.concatenate(
        [fold(pick(over_hot, tokens), width), fold(pick(over_hot, upstream), width)], axis=1
    )
    send[:, 2 * width :] = pick(perm, folded)

    pl.semaphore_wait(barrier, n_expert - 1 + 3)

    started = []

    def push(src, dst, send_sem, recv_sem, device):
        copy = pltpu.make_async_remote_copy(
            src_ref=src,
            dst_ref=dst,
            send_sem=send_sem,
            recv_sem=recv_sem,
            device_id=device,
            device_id_type=MESH,
        )
        copy.start()
        started.append(copy)

    def landed(here, sem):
        pltpu.make_async_copy(here, here, sem).wait()

    for i in range(1, n_expert):
        t = order(i)
        push(send.at[block(t)], got.at[at(0, e)], z_send.at[i - 1], recv.at[e], {"expert": t})
    got[at(0, e), :] = send[block(e), :]

    def arrived(k, s):
        landed(got.at[at(k, s)], recv.at[k * n_expert + s])

    def forward(i):
        s = order(i)
        arrived(1, s)
        arrived(2, s)
        if i % 2 == 0:
            push(got.at[at(1, s)], got.at[at(3, s)], f_send.at[i], recv.at[3 * n_expert + s], {"dp": yn})
        else:
            push(got.at[at(2, s)], got.at[at(3, s)], f_send.at[i], recv.at[3 * n_expert + s], {"dp": xn})

    lag = 2
    for i in range(n_expert):
        s = order(i)
        if i > 0:
            arrived(0, s)
        push(got.at[at(0, s)], got.at[at(1, s)], x_send.at[i], recv.at[n_expert + s], {"dp": xn})
        push(got.at[at(0, s)], got.at[at(2, s)], y_send.at[i], recv.at[2 * n_expert + s], {"dp": yn})
        if i >= lag:
            forward(i - lag)
    for i in range(n_expert - lag, n_expert):
        forward(i)
    for load in loads[3:]:
        load.wait()

    tile = 256

    def work(k, n):
        main = pl.ds(k * group, n * group)
        rest = pl.ds(k * over, n * over)
        tail = pl.ds(mains + k * over, n * over)
        cut = n * group
        for c in range(k, k + n):
            opened = pick(perm, got[pl.ds(c * group, group), 2 * width :])
            extra[pl.ds(c * over, over), :width] = unfold(opened, 0, width)
            extra[pl.ds(c * over, over), width:] = unfold(opened, LANES, width)

        @pl.loop(0, ff // tile)
        def _(f):
            cols = pl.ds(pl.multiple_of(f * tile, tile), tile)
            later = pl.ds(pl.multiple_of(ff + f * tile, tile), tile)
            rows = jnp.concatenate([got[main, :width], extra[rest, :width]], axis=0)
            grads = jnp.concatenate([got[main, width : 2 * width], extra[rest, width:]], axis=0)
            pre = jnp.dot(rows, first[:, cols], preferred_element_type=F32)
            act, slope = gelu_pair(pre)
            act = act.astype(BF)
            ad[main, cols] = act[:cut]
            ad[tail, cols] = act[cut:]
            dact = lax.dot_general(
                grads, second[cols, :], (((1,), (1,)), ((), ())), preferred_element_type=F32
            )
            dpre = (dact * slope).astype(BF)
            ad[main, later] = dpre[:cut]
            ad[tail, later] = dpre[cut:]

        @pl.loop(0, width // tile)
        def _(f):
            cols = pl.ds(pl.multiple_of(f * tile, tile), tile)
            dpre = jnp.concatenate([ad[main, ff:], ad[tail, ff:]], axis=0)
            value = lax.dot_general(
                dpre, first[cols, :], (((1,), (1,)), ((), ())), preferred_element_type=F32
            ).astype(BF)
            part[main, cols] = value[:cut]
            part[tail, cols] = value[cut:]

    far = (1 - upper) * half
    near = upper * half

    def spans(k):
        return (
            pl.ds(pl.multiple_of(k * group + far, half), half),
            pl.ds(mains + k * over, over),
            pl.ds(pl.multiple_of(k * group + near, half), half),
        )

    def slots(k):
        base = (k - 1) * group
        return (
            pl.ds(pl.multiple_of(base + far, half), half),
            pl.ds(3 * group + (k - 1) * over, over),
            pl.ds(pl.multiple_of(base + near, half), half),
        )

    def give(k, device):
        for j, (src, dst) in enumerate(zip(spans(k), slots(k))):
            i = 3 * (k - 1) + j
            push(part.at[src], peer.at[dst], p_send.at[i], p_recv.at[i], {"dp": device})

    work(1, 2)
    give(1, xn)
    give(2, yn)
    for i in range(n_expert):
        arrived(3, order(i))
    work(3, 1)
    give(3, diag)
    work(0, 1)

    def weight_grad(left, left_at, right, right_at, grad, grad_hbm, sems):
        @pl.loop(0, width // tile)
        def _(f):
            cols = pl.ds(pl.multiple_of(left_at + f * tile, tile), tile)
            mine = pl.ds(pl.multiple_of(f * tile, tile), tile)
            tall = jnp.concatenate([left[0][pl.ds(0, mains), cols], left[1][left[2], cols]], axis=0)
            wide = jnp.concatenate(
                [
                    right[0][pl.ds(0, mains), right_at : right_at + width],
                    right[1][right[2], right_at : right_at + width],
                ],
                axis=0,
            )
            grad[mine, :] = lax.dot_general(
                tall, wide, (((0,), (0,)), ((), ())), preferred_element_type=F32
            )
            pltpu.make_async_copy(grad.at[mine], grad_hbm.at[mine], o_sem.at[sems + f]).start()

    rows_all = (got, extra, pl.ds(0, 4 * over))
    hidden_all = (ad, ad, pl.ds(mains, 4 * over))
    weight_grad(hidden_all, 0, rows_all, width, grad_out, grad_out_out, 0)

    def total(j):
        value = part[spans(0)[j], :].astype(F32)
        for k in range(1, 4):
            landed(peer.at[slots(k)[j]], p_recv.at[3 * (k - 1) + j])
            value = value + peer[slots(k)[j], :].astype(F32)
        return value.astype(BF)

    def give_back(i):
        t = order(i)
        push(back_send.at[block(t)], back_got.at[block(e)], b_send.at[i - 1], b_recv.at[e], {"expert": t})

    back_send[pl.ds(pl.multiple_of(far, half), half), :width] = total(0)
    back_send[:, width:] = pick(perm, fold(total(1), width))
    for i in range(n_expert // 2, n_expert):
        give_back(i)
    back_send[pl.ds(pl.multiple_of(near, half), half), :width] = total(2)
    for i in range(1, n_expert // 2):
        give_back(i)
    back_got[block(e), :] = back_send[block(e), :]

    weight_grad(rows_all, 0, hidden_all, ff, grad_in, grad_in_out, 4)

    for i in range(1, n_expert):
        s = order(i)
        landed(back_got.at[block(s)], b_recv.at[s])
    extra_rows = unfold(pick(perm, back_got[:, width:]), 0, width)
    spec = (((0,), (0,)), ((), ()))
    result = lax.dot_general(main_hot, back_got[:, :width], spec, preferred_element_type=F32)
    result = result + lax.dot_general(over_hot, extra_rows, spec, preferred_element_type=F32)
    out_ref[...] = result.astype(BF)
    for copy in started:
        copy.wait_send()
    for f in range(width // tile):
        mine = pl.ds(f * tile, tile)
        pltpu.make_async_copy(grad_out.at[mine], grad_out_out.at[mine], o_sem.at[f]).wait()
        pltpu.make_async_copy(grad_in.at[mine], grad_in_out.at[mine], o_sem.at[4 + f]).wait()


def deliver_kernel(first, second, first_out, second_out, sem):
    rows = first.shape[0] // 4
    copies = []
    for i in range(4):
        here = pl.ds(i * rows, rows)
        copies.append(pltpu.make_async_copy(first.at[here], first_out.at[here], sem.at[2 * i]))
        copies.append(pltpu.make_async_copy(second.at[here], second_out.at[here], sem.at[2 * i + 1]))
    for copy in copies:
        copy.start()
    for copy in copies:
        copy.wait()


def fused_body(tokens, upstream, task_ids, task_expert, w_in, w_out):
    n_expert = lax.axis_size("expert")
    rows_dev, width = tokens.shape
    ff = w_in.shape[2]
    group = n_expert * MAIN
    chunk = group + MAIN
    rows = 4 * chunk
    first, second = w_in[0], w_out[0]
    dma = pltpu.SemaphoreType.DMA
    vmem = pl.BlockSpec(memory_space=pltpu.VMEM)
    smem = pl.BlockSpec(memory_space=pltpu.SMEM)
    hbm = pl.BlockSpec(memory_space=pltpu.HBM)
    free = pl.BlockSpec(memory_space=pl.ANY)
    grads = (
        jax.ShapeDtypeStruct((width, ff), F32),
        jax.ShapeDtypeStruct((ff, width), F32),
    )
    token_grad, grad_in, grad_out = pl.pallas_call(
        functools.partial(exchange_kernel, n_expert, rows_dev, width, ff),
        out_shape=(jax.ShapeDtypeStruct((rows_dev, width), BF),) + grads,
        in_specs=[hbm, hbm, hbm, smem, hbm, hbm],
        out_specs=(vmem, free, free),
        scratch_shapes=[
            pltpu.VMEM((rows_dev, width), BF),
            pltpu.VMEM((rows_dev, width), BF),
            pltpu.VMEM((1, rows_dev), jnp.int32),
            pltpu.VMEM((width, ff), BF),
            pltpu.VMEM((ff, width), BF),
            pltpu.VMEM((group, 2 * width + 2 * LANES), BF),
            pltpu.VMEM((4 * group, 2 * width + 2 * LANES), BF),
            pltpu.VMEM((4 * MAIN, 2 * width), BF),
            pltpu.VMEM((rows, 2 * ff), BF),
            pltpu.VMEM((rows, width), BF),
            pltpu.VMEM((3 * chunk, width), BF),
            pltpu.VMEM((width, ff), F32),
            pltpu.VMEM((ff, width), F32),
            pltpu.VMEM((group, width + LANES), BF),
            pltpu.VMEM((group, width + LANES), BF),
            dma((5,)),
            dma((n_expert - 1,)),
            dma((n_expert,)),
            dma((n_expert,)),
            dma((n_expert,)),
            dma((4 * n_expert,)),
            dma((9,)),
            dma((9,)),
            dma((n_expert - 1,)),
            dma((n_expert,)),
            dma((8,)),
        ],
        compiler_params=pltpu.CompilerParams(
            collective_id=0, has_side_effects=True, vmem_limit_bytes=40 * 1024 * 1024
        ),
        cost_estimate=pl.CostEstimate(
            flops=10 * rows * width * ff, bytes_accessed=12 * width * ff, transcendentals=rows * ff
        ),
    )(tokens, upstream, task_ids.reshape(1, -1), task_expert, first, second)
    grad_in, grad_out = pl.pallas_call(
        deliver_kernel,
        out_shape=grads,
        in_specs=[free, free],
        out_specs=(free, free),
        scratch_shapes=[dma((8,))],
        cost_estimate=pl.CostEstimate(flops=0, bytes_accessed=16 * width * ff, transcendentals=0),
    )(grad_in, grad_out)
    return (token_grad, grad_in[None], grad_out[None])


def general_body(tokens, upstream, task_ids, task_expert, w_in, w_out):
    n_expert = lax.axis_size("expert")
    rows_dev = tokens.shape[0]
    width = tokens.shape[1]
    experts = task_expert.shape[0]
    capacity = max(2, (9 * rows_dev // 8 + n_expert - 1) // n_expert)
    lanes = jnp.arange(experts, dtype=jnp.int32)
    task_hot = (task_ids == lanes[None, :]).astype(jnp.int32)
    target = jnp.sum(task_hot * task_expert[None, :], axis=1)
    dest_hot = (target[:, None] == lanes[None, :]).astype(jnp.int32)
    before = jnp.cumsum(dest_hot, axis=0) - dest_hot
    rank = jnp.sum(before * dest_hot, axis=1)
    slot = target * capacity + rank
    packer = (jnp.arange(experts * capacity, dtype=jnp.int32)[:, None] == slot[None, :]).astype(
        jnp.bfloat16
    )
    send_rows = (
        jnp.dot(packer, tokens, preferred_element_type=jnp.float32)
        .astype(jnp.bfloat16)
        .reshape(experts, capacity, width)
    )
    send_grads = (
        jnp.dot(packer, upstream, preferred_element_type=jnp.float32)
        .astype(jnp.bfloat16)
        .reshape(experts, capacity, width)
    )
    first = w_in[0]
    second = w_out[0]
    got_rows, got_grads = (
        lax.all_to_all(send_rows, "expert", split_axis=0, concat_axis=0, tiled=True),
        lax.all_to_all(send_grads, "expert", split_axis=0, concat_axis=0, tiled=True),
    )
    got_rows = got_rows.reshape(experts * capacity, width)
    got_grads = got_grads.reshape(experts * capacity, width)
    all_rows, all_grads = (
        lax.all_gather(got_rows, "dp", axis=0, tiled=True),
        lax.all_gather(got_grads, "dp", axis=0, tiled=True),
    )
    pre = jnp.dot(all_rows, first, preferred_element_type=jnp.float32)
    act, slope = gelu_pair(pre)
    act = act.astype(jnp.bfloat16)
    grad_second = lax.dot_general(
        act, all_grads, (((0,), (0,)), ((), ())), preferred_element_type=jnp.float32
    )
    dact = lax.dot_general(
        all_grads, second, (((1,), (1,)), ((), ())), preferred_element_type=jnp.float32
    )
    dpre = (dact * slope).astype(jnp.bfloat16)
    grad_first = lax.dot_general(
        all_rows, dpre, (((0,), (0,)), ((), ())), preferred_element_type=jnp.float32
    )
    partial_value = lax.dot_general(
        dpre, first, (((1,), (1,)), ((), ())), preferred_element_type=jnp.float32
    )
    own = lax.psum_scatter(
        partial_value.astype(jnp.bfloat16), "dp", scatter_dimension=0, tiled=True
    ).astype(jnp.float32)
    own = own.astype(jnp.bfloat16).reshape(experts, capacity, width)
    back = lax.all_to_all(own, "expert", split_axis=0, concat_axis=0, tiled=True).reshape(
        experts * capacity, width
    )
    token_grad = lax.dot_general(
        packer, back, (((0,), (0,)), ((), ())), preferred_element_type=jnp.float32
    ).astype(jnp.bfloat16)
    return (token_grad, grad_first[None], grad_second[None])


def body(mesh, tokens, upstream, task_ids, task_expert, w_in, w_out):
    n_expert = mesh.shape["expert"]
    rows_dev, width = tokens.shape
    ff = w_in.shape[2]
    capacity = max(2, (9 * rows_dev // 8 + n_expert - 1) // n_expert)
    fits = (
        mesh.shape["dp"] == 4
        and n_expert == 8
        and rows_dev == 128
        and capacity <= MAIN + 2
        and width == n_expert * LANES
        and ff == width
    )
    run = fused_body if fits else general_body
    return run(tokens, upstream, task_ids, task_expert, w_in, w_out)


def solution(mesh):
    placed = (
        P(("dp", "expert"), None),
        P(("dp", "expert"), None),
        P(("dp", "expert"), None),
        P(),
        P("expert", None, "dp"),
        P("expert", "dp", None),
    )
    return jax.shard_map(
        functools.partial(body, mesh),
        mesh=mesh,
        in_specs=placed,
        out_specs=(P(("dp", "expert"), None), P("expert", None, "dp"), P("expert", "dp", None)),
        check_vma=False,
    )
```

time: 69.3 us -> 320 us (4.62)
  Pallas kernels: 61.2 us -> 308 us
  local copies, waits for them, and re-layouts: 7.19 us -> 11 us
    pallas_call x1, Pallas kernels: 5.58 us -> 255 us  [fused_body(): pl.pallas_call(deliver_kernel, out_shape=grads, in_specs=[free, free], ou...]
    unnamed x12 -> x17, local copies, waits for them, and re-layouts: 7.19 us -> 11 us
where the time goes in v2:
time: 320 us
  Pallas kernels  308 us (96%)
  local copies, waits for them, and re-layouts  11 us (3%)
    pallas_call x1, Pallas kernels, fused_body(): pl.pallas_call(deliver_kernel, out_shape=grads, in_specs=[free, free], ou...  255 us
    pallas_call x1, Pallas kernels, fused_body(): pl.pallas_call(functools.partial(exchange_kernel, n_expert, rows_dev, wid...  53 us
    unnamed x17, local copies, waits for them, and re-layouts  11 us

profile of v2, /device:TPU:0, one launch (start us, length us, event | category | flops | bytes accessed | tf_op | source)
XLA Modules:
  0.0 319.9 jit_solution(2193997835494986175)
XLA Ops:
  0.6 0.0 copy-start.2
  0.6 1.6 copy-done.2
  2.2 0.0 copy-start.3
  2.2 1.6 copy-done.3
  3.8 0.0 copy-start.4
  3.8 0.9 copy-done.4
  4.8 0.0 copy-start.5
  4.8 0.9 copy-done.5
  5.7 0.0 copy-start.6
  5.7 0.7 copy-done.6
  6.4 0.0 copy-start.7
  6.4 0.7 copy-done.7
  7.0 53.0 %shard_map.85 = (bf16[128,1024]{1,0:T(8,128)(2,1)S(1)}, f32[1024,1024]{1,0:T(8,128)S(1)}, f32[1024,1024]{1,0:T(8,128)S(1)}) custom-call(bf16[128,1024]{1,0:T(8,128)(2,1)S(1)} %copy-done.4, bf16[128,1024]{1,0:T(8,128)(2,1)S(1)} %copy-done.5, s32[1,128]{1,0:T(1,128)S(1)} %bitcast.7, s32[8]{0:T(128)S(1)} %copy-done.7, bf16[1024,1024]{1,0:T(8,128)(2,1)S(1)} %bitcast.5, ...), custom_call_target="tpu_custom_call" | custom-call | flops 6039797760 | bytes 12582912 | tf_op jit(solution)/shard_map/pallas_call | solution.py:366
  60.0 0.0 copy-start
  60.0 1.9 copy-done
  62.0 0.0 copy-start.1
  62.0 2.0 copy-done.1
  63.9 255.3 %shard_map.86 = (f32[1024,1024]{1,0:T(8,128)}, f32[1024,1024]{1,0:T(8,128)}) custom-call(f32[1024,1024]{1,0:T(8,128)} %copy-done, f32[1024,1024]{1,0:T(8,128)} %copy-done.1), custom_call_target="tpu_custom_call" | custom-call | bytes 16777216 | tf_op jit(solution)/shard_map/pallas_call | solution.py:406
  319.2 0.7 copy.10
Async XLA Ops:
  0.6 1.6 copy-start.2
  2.2 1.6 copy-start.3
  3.8 0.9 copy-start.4
  4.8 0.9 copy-start.5
  5.7 0.7 copy-start.6
  6.4 0.7 copy-start.7
  60.0 1.9 copy-start
  62.0 2.0 copy-start.1

commit v3 on v2

--- a/solution.py
+++ b/solution.py
@@ -41,7 +41,7 @@
     tokens_hbm,
     upstream_hbm,
     ids_hbm,
-    experts_ref,
+    experts_hbm,
     first_hbm,
     second_hbm,
     out_ref,
@@ -50,6 +50,7 @@
     tokens_ref,
     upstream_ref,
     ids_ref,
+    experts_ref,
     first,
     second,
     send,
@@ -103,6 +104,7 @@
         for i, (src, dst) in enumerate(
             (
                 (ids_hbm, ids_ref),
+                (experts_hbm, experts_ref),
                 (tokens_hbm, tokens_ref),
                 (upstream_hbm, upstream_ref),
                 (first_hbm, first),
@@ -126,6 +128,7 @@
     turned = (row >> 1 & 7) * 16 + (row >> 4) * 2 + (row & 1)
     perm = (turned == col).astype(BF)
     loads[0].wait()
+    loads[1].wait()
     ids = ids_ref[...]
     goal = jnp.zeros(ids.shape, F32)
     for k in range(n_expert):
@@ -140,10 +143,10 @@
     def pick(hot_rows, values):
         return jnp.dot(hot_rows, values, preferred_element_type=F32).astype(BF)
 
-    loads[1].wait()
+    loads[2].wait()
     tokens = tokens_ref[...]
     send[:, :width] = pick(main_hot, tokens)
-    loads[2].wait()
+    loads[3].wait()
     upstream = upstream_ref[...]
     send[:, width : 2 * width] = pick(main_hot, upstream)
     folded = jnp.concatenate(
@@ -198,7 +201,7 @@
             forward(i - lag)
     for i in range(n_expert - lag, n_expert):
         forward(i)
-    for load in loads[3:]:
+    for load in loads[4:]:
         load.wait()
 
     tile = 256
@@ -333,9 +336,9 @@
         pltpu.make_async_copy(grad_in.at[mine], grad_in_out.at[mine], o_sem.at[4 + f]).wait()
 
 
-def deliver_kernel(first, second, first_out, second_out, sem):
+def deliver_kernel(small, first, second, small_out, first_out, second_out, sem):
     rows = first.shape[0] // 4
-    copies = []
+    copies = [pltpu.make_async_copy(small, small_out, sem.at[8])]
     for i in range(4):
         here = pl.ds(i * rows, rows)
         copies.append(pltpu.make_async_copy(first.at[here], first_out.at[here], sem.at[2 * i]))
@@ -356,22 +359,24 @@
     first, second = w_in[0], w_out[0]
     dma = pltpu.SemaphoreType.DMA
     vmem = pl.BlockSpec(memory_space=pltpu.VMEM)
-    smem = pl.BlockSpec(memory_space=pltpu.SMEM)
     hbm = pl.BlockSpec(memory_space=pltpu.HBM)
     free = pl.BlockSpec(memory_space=pl.ANY)
-    grads = (
+    results = (
+        jax.ShapeDtypeStruct((rows_dev, width), BF),
         jax.ShapeDtypeStruct((width, ff), F32),
         jax.ShapeDtypeStruct((ff, width), F32),
     )
+    held = (tokens, upstream, task_ids.reshape(1, -1), task_expert, first, second)
     token_grad, grad_in, grad_out = pl.pallas_call(
         functools.partial(exchange_kernel, n_expert, rows_dev, width, ff),
-        out_shape=(jax.ShapeDtypeStruct((rows_dev, width), BF),) + grads,
-        in_specs=[hbm, hbm, hbm, smem, hbm, hbm],
+        out_shape=results,
+        in_specs=[hbm] * 6,
         out_specs=(vmem, free, free),
         scratch_shapes=[
             pltpu.VMEM((rows_dev, width), BF),
             pltpu.VMEM((rows_dev, width), BF),
             pltpu.VMEM((1, rows_dev), jnp.int32),
+            pltpu.SMEM(task_expert.shape, jnp.int32),
             pltpu.VMEM((width, ff), BF),
             pltpu.VMEM((ff, width), BF),
             pltpu.VMEM((group, 2 * width + 2 * LANES), BF),
@@ -384,7 +389,7 @@
             pltpu.VMEM((ff, width), F32),
             pltpu.VMEM((group, width + LANES), BF),
             pltpu.VMEM((group, width + LANES), BF),
-            dma((5,)),
+            dma((6,)),
             dma((n_expert - 1,)),
             dma((n_expert,)),
             dma((n_expert,)),
@@ -402,15 +407,16 @@
         cost_estimate=pl.CostEstimate(
             flops=10 * rows * width * ff, bytes_accessed=12 * width * ff, transcendentals=rows * ff
         ),
-    )(tokens, upstream, task_ids.reshape(1, -1), task_expert, first, second)
-    grad_in, grad_out = pl.pallas_call(
+    )(*(pltpu.with_memory_space_constraint(x, pltpu.HBM) for x in held))
+    token_grad, grad_in, grad_out = pl.pallas_call(
         deliver_kernel,
-        out_shape=grads,
-        in_specs=[free, free],
-        out_specs=(free, free),
-        scratch_shapes=[dma((8,))],
+        out_shape=results,
+        in_specs=[free, free, free],
+        out_specs=(free, free, free),
+        scratch_shapes=[dma((9,))],
+        compiler_params=pltpu.CompilerParams(vmem_limit_bytes=1024 * 1024),
         cost_estimate=pl.CostEstimate(flops=0, bytes_accessed=16 * width * ff, transcendentals=0),
-    )(grad_in, grad_out)
+    )(token_grad, grad_in, grad_out)
     return (token_grad, grad_in[None], grad_out[None])
 
 

time: 320 us -> 56.4 us (0.18)
  Pallas kernels: 308 us -> 55.6 us
  local copies, waits for them, and re-layouts: 11 us -> 0 us
    pallas_call x1, Pallas kernels: 255 us -> 3.46 us  [fused_body(): pl.pallas_call(deliver_kernel, out_shape=results, in_specs=[free, free, f...]
    unnamed x17 -> x0, local copies, waits for them, and re-layouts: 11 us -> none
where the time goes in v3:
time: 56.4 us; the launch traced here: 56.3 us
  Pallas kernels  55.6 us (99%)
  between operations  0.64 us (1%)
    pallas_call x1, Pallas kernels, fused_body(): pl.pallas_call(functools.partial(exchange_kernel, n_expert, rows_dev, wid...  52.2 us
    pallas_call x1, Pallas kernels, fused_body(): pl.pallas_call(deliver_kernel, out_shape=results, in_specs=[free, free, f...  3.46 us

profile of v3, /device:TPU:0, one launch (start us, length us, event | category | flops | bytes accessed | tf_op | source)
XLA Modules:
  0.0 56.3 jit_solution(8906427752018774602)
XLA Ops:
  0.6 52.2 %shard_map.85 = (bf16[128,1024]{1,0:T(8,128)(2,1)S(1)}, f32[1024,1024]{1,0:T(8,128)S(1)}, f32[1024,1024]{1,0:T(8,128)S(1)}) custom-call(bf16[128,1024]{1,0:T(8,128)(2,1)} %tokens_hbm.1, bf16[128,1024]{1,0:T(8,128)(2,1)} %upstream_hbm.1, s32[1,128]{1,0:T(1,128)} %bitcast.9, s32[8]{0:T(128)} %experts_hbm.1, bf16[1024,1024]{1,0:T(8,128)(2,1)} %bitcast.7, ...), custom_call_target="tpu_custom_call" | custom-call | flops 6039797760 | bytes 12582912 | tf_op jit(solution)/shard_map/pallas_call | solution.py:370
  52.8 3.5 %shard_map.86 = (bf16[128,1024]{1,0:T(8,128)(2,1)}, f32[1024,1024]{1,0:T(8,128)}, f32[1024,1024]{1,0:T(8,128)}) custom-call(bf16[128,1024]{1,0:T(8,128)(2,1)S(1)} %get-tuple-element.9.small, f32[1024,1024]{1,0:T(8,128)S(1)} %get-tuple-element.10.first, f32[1024,1024]{1,0:T(8,128)S(1)} %get-tuple-element.11.second), custom_call_target="tpu_custom_call" | custom-call | bytes 16777216 | tf_op jit(solution)/shard_map/pallas_call | solution.py:411

commit v4 on v3

--- a/solution.py
+++ b/solution.py
@@ -58,7 +58,9 @@
     extra,
     ad,
     part,
-    peer,
+    middle,
+    peer_x,
+    peer_y,
     grad_in,
     grad_out,
     back_send,
@@ -79,6 +81,7 @@
     group = n_expert * MAIN
     over = MAIN
     half = group // 2
+    chunk = group + over
     mains = 4 * group
     e = lax.axis_index("expert")
     d = lax.axis_index("dp")
@@ -241,40 +244,46 @@
             value = lax.dot_general(
                 dpre, first[cols, :], (((1,), (1,)), ((), ())), preferred_element_type=F32
             ).astype(BF)
-            part[main, cols] = value[:cut]
-            part[tail, cols] = value[cut:]
+            for c in range(n):
+                base = (k + c) * chunk
+                low = pl.multiple_of(base + (1 - upper) * (half + over), over)
+                high = pl.multiple_of(base + upper * (half + over), over)
+                part[pl.ds(low, half), cols] = value[c * group : c * group + half]
+                part[pl.ds(high, half), cols] = value[c * group + half : (c + 1) * group]
+                part[pl.ds(base + half, over), cols] = value[cut + c * over : cut + (c + 1) * over]
 
     far = (1 - upper) * half
     near = upper * half
-
-    def spans(k):
-        return (
-            pl.ds(pl.multiple_of(k * group + far, half), half),
-            pl.ds(mains + k * over, over),
-            pl.ds(pl.multiple_of(k * group + near, half), half),
+    spans = ((0, half + over), (half + over, half))
+    left, right = pl.ds(0, width // 2), pl.ds(width // 2, width // 2)
+
+    def give(k, low, size, cols, dst, i, device):
+        push(
+            part.at[pl.ds(k * chunk + low, size), cols],
+            dst.at[pl.ds(low, size), cols],
+            p_send.at[i],
+            p_recv.at[i],
+            {"dp": device},
         )
 
-    def slots(k):
-        base = (k - 1) * group
-        return (
-            pl.ds(pl.multiple_of(base + far, half), half),
-            pl.ds(3 * group + (k - 1) * over, over),
-            pl.ds(pl.multiple_of(base + near, half), half),
-        )
-
-    def give(k, device):
-        for j, (src, dst) in enumerate(zip(spans(k), slots(k))):
-            i = 3 * (k - 1) + j
-            push(part.at[src], peer.at[dst], p_send.at[i], p_recv.at[i], {"dp": device})
-
     work(1, 2)
-    give(1, xn)
-    give(2, yn)
+    give(1, 0, chunk, left, peer_x, 0, xn)
+    give(2, 0, chunk, right, peer_y, 1, yn)
     for i in range(n_expert):
         arrived(3, order(i))
     work(3, 1)
-    give(3, diag)
+    for j, (low, size) in enumerate(spans):
+        give(3, low, size, left, middle, 2 + 2 * j, xn)
+        give(3, low, size, right, middle, 3 + 2 * j, yn)
     work(0, 1)
+    for j, (low, size) in enumerate(spans):
+        here = pl.ds(low, size)
+        for k, cols, dst, near_dev, m in ((2, left, peer_y, yn, 0), (1, right, peer_x, xn, 1)):
+            mine = pl.ds(k * chunk + low, size)
+            landed(middle.at[here, cols], p_recv.at[2 + 2 * j + m])
+            value = part[mine, cols].astype(F32) + middle[here, cols].astype(F32)
+            part[mine, cols] = value.astype(BF)
+            give(k, low, size, cols, dst, 6 + 2 * j + m, near_dev)
 
     def weight_grad(left, left_at, right, right_at, grad, grad_hbm, sems):
         @pl.loop(0, width // tile)
@@ -298,22 +307,27 @@
     hidden_all = (ad, ad, pl.ds(mains, 4 * over))
     weight_grad(hidden_all, 0, rows_all, width, grad_out, grad_out_out, 0)
 
+    landed(peer_x.at[pl.ds(0, chunk), left], p_recv.at[0])
+    landed(peer_y.at[pl.ds(0, chunk), right], p_recv.at[1])
+
     def total(j):
-        value = part[spans(0)[j], :].astype(F32)
-        for k in range(1, 4):
-            landed(peer.at[slots(k)[j]], p_recv.at[3 * (k - 1) + j])
-            value = value + peer[slots(k)[j], :].astype(F32)
+        low, size = spans[j]
+        here = pl.ds(low, size)
+        landed(peer_y.at[here, left], p_recv.at[6 + 2 * j])
+        landed(peer_x.at[here, right], p_recv.at[7 + 2 * j])
+        value = part[here, :].astype(F32) + peer_x[here, :].astype(F32) + peer_y[here, :].astype(F32)
         return value.astype(BF)
 
     def give_back(i):
         t = order(i)
         push(back_send.at[block(t)], back_got.at[block(e)], b_send.at[i - 1], b_recv.at[e], {"expert": t})
 
-    back_send[pl.ds(pl.multiple_of(far, half), half), :width] = total(0)
-    back_send[:, width:] = pick(perm, fold(total(1), width))
+    first_rows = total(0)
+    back_send[pl.ds(pl.multiple_of(far, half), half), :width] = first_rows[:half]
+    back_send[:, width:] = pick(perm, fold(first_rows[half:], width))
     for i in range(n_expert // 2, n_expert):
         give_back(i)
-    back_send[pl.ds(pl.multiple_of(near, half), half), :width] = total(2)
+    back_send[pl.ds(pl.multiple_of(near, half), half), :width] = total(1)
     for i in range(1, n_expert // 2):
         give_back(i)
     back_got[block(e), :] = back_send[block(e), :]
@@ -384,7 +398,9 @@
             pltpu.VMEM((4 * MAIN, 2 * width), BF),
             pltpu.VMEM((rows, 2 * ff), BF),
             pltpu.VMEM((rows, width), BF),
-            pltpu.VMEM((3 * chunk, width), BF),
+            pltpu.VMEM((chunk, width), BF),
+            pltpu.VMEM((chunk, width), BF),
+            pltpu.VMEM((chunk, width), BF),
             pltpu.VMEM((width, ff), F32),
             pltpu.VMEM((ff, width), F32),
             pltpu.VMEM((group, width + LANES), BF),
@@ -395,8 +411,8 @@
             dma((n_expert,)),
             dma((n_expert,)),
             dma((4 * n_expert,)),
-            dma((9,)),
-            dma((9,)),
+            dma((10,)),
+            dma((10,)),
             dma((n_expert - 1,)),
             dma((n_expert,)),
             dma((8,)),

time: 56.4 us -> 56.8 us (level)
  no operation moved by 1% of the time
where the time goes in v4:
time: 56.8 us; the launch traced here: 56.7 us
  Pallas kernels  56 us (99%)
  between operations  0.64 us (1%)
    pallas_call x1, Pallas kernels, fused_body(): pl.pallas_call(functools.partial(exchange_kernel, n_expert, rows_dev, wid...  52.6 us
    pallas_call x1, Pallas kernels, fused_body(): pl.pallas_call(deliver_kernel, out_shape=results, in_specs=[free, free, f...  3.46 us

profile of v4, /device:TPU:0, one launch (start us, length us, event | category | flops | bytes accessed | tf_op | source)
XLA Modules:
  0.0 56.7 jit_solution(8440690628945517011)
XLA Ops:
  0.6 52.6 %shard_map.85 = (bf16[128,1024]{1,0:T(8,128)(2,1)S(1)}, f32[1024,1024]{1,0:T(8,128)S(1)}, f32[1024,1024]{1,0:T(8,128)S(1)}) custom-call(bf16[128,1024]{1,0:T(8,128)(2,1)} %tokens_hbm.1, bf16[128,1024]{1,0:T(8,128)(2,1)} %upstream_hbm.1, s32[1,128]{1,0:T(1,128)} %bitcast.9, s32[8]{0:T(128)} %experts_hbm.1, bf16[1024,1024]{1,0:T(8,128)(2,1)} %bitcast.7, ...), custom_call_target="tpu_custom_call" | custom-call | flops 6039797760 | bytes 12582912 | tf_op jit(solution)/shard_map/pallas_call | solution.py:384
  53.2 3.5 %shard_map.86 = (bf16[128,1024]{1,0:T(8,128)(2,1)}, f32[1024,1024]{1,0:T(8,128)}, f32[1024,1024]{1,0:T(8,128)}) custom-call(bf16[128,1024]{1,0:T(8,128)(2,1)S(1)} %get-tuple-element.9.small, f32[1024,1024]{1,0:T(8,128)S(1)} %get-tuple-element.10.first, f32[1024,1024]{1,0:T(8,128)S(1)} %get-tuple-element.11.second), custom_call_target="tpu_custom_call" | custom-call | bytes 16777216 | tf_op jit(solution)/shard_map/pallas_call | solution.py:427

commit v5 on v4

--- a/solution.py
+++ b/solution.py
@@ -202,62 +202,75 @@
         push(got.at[at(0, s)], got.at[at(2, s)], y_send.at[i], recv.at[2 * n_expert + s], {"dp": yn})
         if i >= lag:
             forward(i - lag)
-    for i in range(n_expert - lag, n_expert):
-        forward(i)
     for load in loads[4:]:
         load.wait()
 
     tile = 256
-
-    def work(k, n):
-        main = pl.ds(k * group, n * group)
-        rest = pl.ds(k * over, n * over)
-        tail = pl.ds(mains + k * over, n * over)
-        cut = n * group
-        for c in range(k, k + n):
+    far = (1 - upper) * half
+    near = upper * half
+    spans = ((0, half + over), (half + over, half))
+
+    def work(pieces, spilled, stops, between):
+        mine = [pl.ds(pl.multiple_of(c * group + (near if j else far), half), half) for c, j in pieces]
+        cut = half * len(pieces)
+        if spilled:
+            rest = pl.ds(spilled[0] * over, len(spilled) * over)
+            tail = pl.ds(mains + spilled[0] * over, len(spilled) * over)
+        for c in spilled:
             opened = pick(perm, got[pl.ds(c * group, group), 2 * width :])
             extra[pl.ds(c * over, over), :width] = unfold(opened, 0, width)
             extra[pl.ds(c * over, over), width:] = unfold(opened, LANES, width)
 
-        @pl.loop(0, ff // tile)
-        def _(f):
+        def joined(main, more, cols):
+            parts = [main[rows, cols] for rows in mine]
+            return jnp.concatenate(parts + ([more[0][more[1], cols]] if spilled else []), axis=0)
+
+        def spread(value, cols):
+            for n, rows in enumerate(mine):
+                ad[rows, cols] = value[n * half : (n + 1) * half]
+            if spilled:
+                ad[tail, cols] = value[cut:]
+
+        more = (extra, rest) if spilled else None
+        later_more = (ad, tail) if spilled else None
+
+        def hidden(f):
             cols = pl.ds(pl.multiple_of(f * tile, tile), tile)
             later = pl.ds(pl.multiple_of(ff + f * tile, tile), tile)
-            rows = jnp.concatenate([got[main, :width], extra[rest, :width]], axis=0)
-            grads = jnp.concatenate([got[main, width : 2 * width], extra[rest, width:]], axis=0)
+            rows = joined(got, more, pl.ds(0, width))
+            grads = joined(got, more, pl.ds(width, width))
             pre = jnp.dot(rows, first[:, cols], preferred_element_type=F32)
             act, slope = gelu_pair(pre)
-            act = act.astype(BF)
-            ad[main, cols] = act[:cut]
-            ad[tail, cols] = act[cut:]
+            spread(act.astype(BF), cols)
             dact = lax.dot_general(
                 grads, second[cols, :], (((1,), (1,)), ((), ())), preferred_element_type=F32
             )
-            dpre = (dact * slope).astype(BF)
-            ad[main, later] = dpre[:cut]
-            ad[tail, later] = dpre[cut:]
+            spread((dact * slope).astype(BF), later)
+
+        low = 0
+        for high, then in stops:
+            pl.loop(low, high)(hidden)
+            then()
+            low = high
+        pl.loop(low, ff // tile)(hidden)
+        between()
 
         @pl.loop(0, width // tile)
         def _(f):
             cols = pl.ds(pl.multiple_of(f * tile, tile), tile)
-            dpre = jnp.concatenate([ad[main, ff:], ad[tail, ff:]], axis=0)
+            dpre = joined(ad, later_more, pl.ds(ff, ff))
             value = lax.dot_general(
                 dpre, first[cols, :], (((1,), (1,)), ((), ())), preferred_element_type=F32
             ).astype(BF)
-            for c in range(n):
-                base = (k + c) * chunk
-                low = pl.multiple_of(base + (1 - upper) * (half + over), over)
-                high = pl.multiple_of(base + upper * (half + over), over)
-                part[pl.ds(low, half), cols] = value[c * group : c * group + half]
-                part[pl.ds(high, half), cols] = value[c * group + half : (c + 1) * group]
-                part[pl.ds(base + half, over), cols] = value[cut + c * over : cut + (c + 1) * over]
-
-    far = (1 - upper) * half
-    near = upper * half
-    spans = ((0, half + over), (half + over, half))
+            for n, (c, j) in enumerate(pieces):
+                part[pl.ds(c * chunk + spans[j][0], half), cols] = value[n * half : (n + 1) * half]
+            for n, c in enumerate(spilled):
+                part[pl.ds(c * chunk + half, over), cols] = value[cut + n * over : cut + (n + 1) * over]
+
     left, right = pl.ds(0, width // 2), pl.ds(width // 2, width // 2)
 
-    def give(k, low, size, cols, dst, i, device):
+    def give(k, j, cols, dst, i, device):
+        low, size = spans[j]
         push(
             part.at[pl.ds(k * chunk + low, size), cols],
             dst.at[pl.ds(low, size), cols],
@@ -266,24 +279,36 @@
             {"dp": device},
         )
 
-    work(1, 2)
-    give(1, 0, chunk, left, peer_x, 0, xn)
-    give(2, 0, chunk, right, peer_y, 1, yn)
-    for i in range(n_expert):
-        arrived(3, order(i))
-    work(3, 1)
-    for j, (low, size) in enumerate(spans):
-        give(3, low, size, left, middle, 2 + 2 * j, xn)
-        give(3, low, size, right, middle, 3 + 2 * j, yn)
-    work(0, 1)
-    for j, (low, size) in enumerate(spans):
+    def give_all(j):
+        give(3, j, left, middle, 6 * j, xn)
+        give(3, j, right, middle, 6 * j + 1, yn)
+        give(1, j, left, peer_x, 6 * j + 2, xn)
+        give(2, j, right, peer_y, 6 * j + 3, yn)
+
+    def relay(j):
+        low, size = spans[j]
         here = pl.ds(low, size)
-        for k, cols, dst, near_dev, m in ((2, left, peer_y, yn, 0), (1, right, peer_x, xn, 1)):
+        for k, cols, dst, device, m in ((2, left, peer_y, yn, 0), (1, right, peer_x, xn, 1)):
             mine = pl.ds(k * chunk + low, size)
-            landed(middle.at[here, cols], p_recv.at[2 + 2 * j + m])
+            landed(middle.at[here, cols], p_recv.at[6 * j + m])
             value = part[mine, cols].astype(F32) + middle[here, cols].astype(F32)
             part[mine, cols] = value.astype(BF)
-            give(k, low, size, cols, dst, 6 + 2 * j + m, near_dev)
+            give(k, j, cols, dst, 6 * j + 4 + m, device)
+
+    def nothing():
+        pass
+
+    for i in range(n_expert // 2):
+        arrived(3, order(i))
+    stops = ((1, lambda: forward(n_expert - 2)), (2, lambda: forward(n_expert - 1)))
+    work(((1, 1), (2, 1), (3, 1)), (), stops, nothing)
+    give_all(1)
+    for i in range(n_expert // 2, n_expert):
+        arrived(3, order(i))
+    work(((1, 0), (2, 0), (3, 0)), (1, 2, 3), (), lambda: relay(1))
+    give_all(0)
+    work(((0, 0), (0, 1)), (0,), (), nothing)
+    relay(0)
 
     def weight_grad(left, left_at, right, right_at, grad, grad_hbm, sems):
         @pl.loop(0, width // tile)
@@ -303,32 +328,30 @@
             )
             pltpu.make_async_copy(grad.at[mine], grad_hbm.at[mine], o_sem.at[sems + f]).start()
 
-    rows_all = (got, extra, pl.ds(0, 4 * over))
-    hidden_all = (ad, ad, pl.ds(mains, 4 * over))
-    weight_grad(hidden_all, 0, rows_all, width, grad_out, grad_out_out, 0)
-
-    landed(peer_x.at[pl.ds(0, chunk), left], p_recv.at[0])
-    landed(peer_y.at[pl.ds(0, chunk), right], p_recv.at[1])
-
     def total(j):
         low, size = spans[j]
         here = pl.ds(low, size)
-        landed(peer_y.at[here, left], p_recv.at[6 + 2 * j])
-        landed(peer_x.at[here, right], p_recv.at[7 + 2 * j])
+        landed(peer_x.at[here, left], p_recv.at[6 * j + 2])
+        landed(peer_y.at[here, right], p_recv.at[6 * j + 3])
+        landed(peer_y.at[here, left], p_recv.at[6 * j + 4])
+        landed(peer_x.at[here, right], p_recv.at[6 * j + 5])
         value = part[here, :].astype(F32) + peer_x[here, :].astype(F32) + peer_y[here, :].astype(F32)
         return value.astype(BF)
+
+    rows_all = (got, extra, pl.ds(0, 4 * over))
+    hidden_all = (ad, ad, pl.ds(mains, 4 * over))
+    near_rows = total(1)
+    back_send[pl.ds(pl.multiple_of(near, half), half), :width] = near_rows
+    weight_grad(hidden_all, 0, rows_all, width, grad_out, grad_out_out, 0)
+    far_rows = total(0)
+    back_send[pl.ds(pl.multiple_of(far, half), half), :width] = far_rows[:half]
+    back_send[:, width:] = pick(perm, fold(far_rows[half:], width))
 
     def give_back(i):
         t = order(i)
         push(back_send.at[block(t)], back_got.at[block(e)], b_send.at[i - 1], b_recv.at[e], {"expert": t})
 
-    first_rows = total(0)
-    back_send[pl.ds(pl.multiple_of(far, half), half), :width] = first_rows[:half]
-    back_send[:, width:] = pick(perm, fold(first_rows[half:], width))
-    for i in range(n_expert // 2, n_expert):
-        give_back(i)
-    back_send[pl.ds(pl.multiple_of(near, half), half), :width] = total(1)
-    for i in range(1, n_expert // 2):
+    for i in range(n_expert - 1, 0, -1):
         give_back(i)
     back_got[block(e), :] = back_send[block(e), :]
 
@@ -411,8 +434,8 @@
             dma((n_expert,)),
             dma((n_expert,)),
             dma((4 * n_expert,)),
-            dma((10,)),
-            dma((10,)),
+            dma((12,)),
+            dma((12,)),
             dma((n_expert - 1,)),
             dma((n_expert,)),
             dma((8,)),

time: 56.8 us -> 56.1 us (0.988)
  Pallas kernels: 56 us -> 55.3 us
    pallas_call x1, Pallas kernels: 52.6 us -> 51.8 us  [fused_body(): pl.pallas_call(functools.partial(exchange_kernel, n_expert, rows_dev, wid...]
where the time goes in v5:
time: 56.1 us; the launch traced here: 55.9 us
  Pallas kernels  55.3 us (99%)
  between operations  0.64 us (1%)
    pallas_call x1, Pallas kernels, fused_body(): pl.pallas_call(functools.partial(exchange_kernel, n_expert, rows_dev, wid...  51.8 us
    pallas_call x1, Pallas kernels, fused_body(): pl.pallas_call(deliver_kernel, out_shape=results, in_specs=[free, free, f...  3.46 us

profile of v5, /device:TPU:0, one launch (start us, length us, event | category | flops | bytes accessed | tf_op | source)
XLA Modules:
  0.0 55.9 jit_solution(12082632566497005739)
XLA Ops:
  0.6 51.8 %shard_map.85 = (bf16[128,1024]{1,0:T(8,128)(2,1)S(1)}, f32[1024,1024]{1,0:T(8,128)S(1)}, f32[1024,1024]{1,0:T(8,128)S(1)}) custom-call(bf16[128,1024]{1,0:T(8,128)(2,1)} %tokens_hbm.1, bf16[128,1024]{1,0:T(8,128)(2,1)} %upstream_hbm.1, s32[1,128]{1,0:T(1,128)} %bitcast.9, s32[8]{0:T(128)} %experts_hbm.1, bf16[1024,1024]{1,0:T(8,128)(2,1)} %bitcast.7, ...), custom_call_target="tpu_custom_call" | custom-call | flops 6039797760 | bytes 12582912 | tf_op jit(solution)/shard_map/pallas_call | solution.py:407
  52.4 3.5 %shard_map.86 = (bf16[128,1024]{1,0:T(8,128)(2,1)}, f32[1024,1024]{1,0:T(8,128)}, f32[1024,1024]{1,0:T(8,128)}) custom-call(bf16[128,1024]{1,0:T(8,128)(2,1)S(1)} %get-tuple-element.9.small, f32[1024,1024]{1,0:T(8,128)S(1)} %get-tuple-element.10.first, f32[1024,1024]{1,0:T(8,128)S(1)} %get-tuple-element.11.second), custom_call_target="tpu_custom_call" | custom-call | bytes 16777216 | tf_op jit(solution)/shard_map/pallas_call | solution.py:450

commit v6 on v5

--- a/solution.py
+++ b/solution.py
@@ -176,6 +176,8 @@
     def landed(here, sem):
         pltpu.make_async_copy(here, here, sem).wait()
 
+    push(send.at[block(e)], got.at[at(1, e)], x_send.at[0], recv.at[n_expert + e], {"dp": xn})
+    push(send.at[block(e)], got.at[at(2, e)], y_send.at[0], recv.at[2 * n_expert + e], {"dp": yn})
     for i in range(1, n_expert):
         t = order(i)
         push(send.at[block(t)], got.at[at(0, e)], z_send.at[i - 1], recv.at[e], {"expert": t})
@@ -194,10 +196,9 @@
             push(got.at[at(2, s)], got.at[at(3, s)], f_send.at[i], recv.at[3 * n_expert + s], {"dp": xn})
 
     lag = 2
-    for i in range(n_expert):
+    for i in range(1, n_expert):
         s = order(i)
-        if i > 0:
-            arrived(0, s)
+        arrived(0, s)
         push(got.at[at(0, s)], got.at[at(1, s)], x_send.at[i], recv.at[n_expert + s], {"dp": xn})
         push(got.at[at(0, s)], got.at[at(2, s)], y_send.at[i], recv.at[2 * n_expert + s], {"dp": yn})
         if i >= lag:

time: 56.1 us -> 56 us (level)
  no operation moved by 1% of the time
where the time goes in v6:
time: 56 us; the launch traced here: 55.9 us
  Pallas kernels  55.3 us (99%)
  between operations  0.64 us (1%)
    pallas_call x1, Pallas kernels, fused_body(): pl.pallas_call(functools.partial(exchange_kernel, n_expert, rows_dev, wid...  51.8 us
    pallas_call x1, Pallas kernels, fused_body(): pl.pallas_call(deliver_kernel, out_shape=results, in_specs=[free, free, f...  3.46 us

profile of v6, /device:TPU:0, one launch (start us, length us, event | category | flops | bytes accessed | tf_op | source)
XLA Modules:
  0.0 55.9 jit_solution(9702220491613539806)
XLA Ops:
  0.6 51.8 %shard_map.85 = (bf16[128,1024]{1,0:T(8,128)(2,1)S(1)}, f32[1024,1024]{1,0:T(8,128)S(1)}, f32[1024,1024]{1,0:T(8,128)S(1)}) custom-call(bf16[128,1024]{1,0:T(8,128)(2,1)} %tokens_hbm.1, bf16[128,1024]{1,0:T(8,128)(2,1)} %upstream_hbm.1, s32[1,128]{1,0:T(1,128)} %bitcast.9, s32[8]{0:T(128)} %experts_hbm.1, bf16[1024,1024]{1,0:T(8,128)(2,1)} %bitcast.7, ...), custom_call_target="tpu_custom_call" | custom-call | flops 6039797760 | bytes 12582912 | tf_op jit(solution)/shard_map/pallas_call | solution.py:408
  52.4 3.5 %shard_map.86 = (bf16[128,1024]{1,0:T(8,128)(2,1)}, f32[1024,1024]{1,0:T(8,128)}, f32[1024,1024]{1,0:T(8,128)}) custom-call(bf16[128,1024]{1,0:T(8,128)(2,1)S(1)} %get-tuple-element.9.small, f32[1024,1024]{1,0:T(8,128)S(1)} %get-tuple-element.10.first, f32[1024,1024]{1,0:T(8,128)S(1)} %get-tuple-element.11.second), custom_call_target="tpu_custom_call" | custom-call | bytes 16777216 | tf_op jit(solution)/shard_map/pallas_call | solution.py:451
